TPU v7x, 256 devices: a whole 4x4x8 slice. The times are simulated.
256 devices in a mesh: list: 64 (over z_lo, y, x, core), row: 4 (over z_hi).
Axes of the slice: x: 4, y: 4, z: 8 (z_hi: 4, z_lo: 2; z = z_hi * 2 + z_lo), core: 2. Of those that a mesh axis runs over, the one named last changes fastest.
Arguments:
- corpus: bfloat16 [262144, 768], P(('list', 'row')), may hold values from -6 to 6
- row_list: int32 [262144], P(('list', 'row')), may hold values from 0 to 4095, as said below
- list_slot: int32 [4096], replicated, may hold values from 0 to 4095, as said below
- member_counts: int32 [4096], P('list'), may hold values from 32 to 96, as said below
- old_centroids: float32 [4096, 768], P('list'), may hold values from -6 to 6
- next_rows: bfloat16 [393216, 768], P(('list', 'row')), may hold values from -6 to 6
Outputs:
- new_centroids: float32 [4096, 768], P('list')
- best_score: float32 [393216], P(('list', 'row'))
Inputs may be any that keep to these rules, and one draw needn't show every extreme that they name: `row_list`: each device sends every owner (list_slot // 64) at least 8 and at most 24 of its rows; some owner receives 24 rows from every device. `list_slot`: A permutation of the list numbers. `member_counts`: the exact number of corpus rows in each slot's list; the lists of one owner differ by at most one.
All inputs are finite; a program needn't handle non-finite values.
Results may differ from a plain program's by a relative error of at most 0.0025.
Values may be sent and summed in bfloat16 or wider, within the bound.
A program may use at most 64 MiB of HBM per device.

v0:
```python
import jax
import jax.numpy as jnp
from jax import lax
from jax.sharding import PartitionSpec as P

ITERS = 3
eps_norm = 1e-06
aniso_par = 32.0
perp_weight = 1.0
prior_weight = 16.0


def unit_of(row_block):
    values = row_block.astype(jnp.float32)
    scaled = values / jnp.sqrt(jnp.sum(values * values, axis=1, keepdims=True) + eps_norm)
    return scaled.astype(jnp.bfloat16)


def split_pair(values):
    high_part = values.astype(jnp.bfloat16)
    low_part = (values - high_part.astype(jnp.float32)).astype(jnp.bfloat16)
    return (high_part, low_part)


def prepare(member_block, member_local, lists_own):
    unit_rows = unit_of(member_block)
    membership = (member_local[:, None] == jnp.arange(lists_own, dtype=jnp.int32)[None, :]).astype(
        jnp.float32
    )
    return (unit_rows, membership)


def gram_part(unit_rows, membership, vectors):
    inner_dims = (((1,), (1,)), ((), ()))
    outer_dims = (((0,), (0,)), ((), ()))
    vec_high, vec_low = split_pair(vectors)
    scores = lax.dot_general(unit_rows, vec_high, inner_dims, preferred_element_type=jnp.float32)
    scores = scores + lax.dot_general(
        unit_rows, vec_low, inner_dims, preferred_element_type=jnp.float32
    )
    weighted = scores * membership
    wgt_high, wgt_low = split_pair(weighted)
    result = lax.dot_general(wgt_high, unit_rows, outer_dims, preferred_element_type=jnp.float32)
    return result + lax.dot_general(
        wgt_low, unit_rows, outer_dims, preferred_element_type=jnp.float32
    )


def member_total(membership, member_block):
    return lax.dot_general(
        membership.astype(jnp.bfloat16),
        member_block,
        (((0,), (0,)), ((), ())),
        preferred_element_type=jnp.float32,
    )


def on_device(corpus, row_list, list_slot, member_counts, old_centroids, next_rows):
    n_owner = lax.axis_size("list")
    lists_own = old_centroids.shape[0]
    local_rows = corpus.shape[0]
    cap_slots = 3 * local_rows // (2 * n_owner)
    width = corpus.shape[1]
    slot_ids = jnp.take(list_slot, row_list)
    owner_id = slot_ids // lists_own
    local_id = slot_ids % lists_own
    hits = (owner_id[:, None] == jnp.arange(n_owner, dtype=jnp.int32)[None, :]).astype(jnp.int32)
    rank_in = jnp.sum((jnp.cumsum(hits, axis=0) - 1) * hits, axis=1)
    dest_idx = owner_id * cap_slots + rank_in
    send_rows = (
        jnp.zeros((n_owner * cap_slots, width), jnp.bfloat16)
        .at[dest_idx]
        .set(corpus)
        .reshape(n_owner, cap_slots, width)
    )
    send_local = (
        jnp.full((n_owner * cap_slots,), -1, jnp.int32)
        .at[dest_idx]
        .set(local_id)
        .reshape(n_owner, cap_slots)
    )
    recv_rows, recv_local = (
        lax.all_to_all(send_rows, "list", split_axis=0, concat_axis=0, tiled=True),
        lax.all_to_all(send_local, "list", split_axis=0, concat_axis=0, tiled=True),
    )
    recv_rows = recv_rows.reshape(n_owner * cap_slots, width)
    recv_local = recv_local.reshape(n_owner * cap_slots)
    centroids = old_centroids
    unit_rows, membership = prepare(recv_rows, recv_local, lists_own)
    row_sums, first_gram = lax.psum(
        (member_total(membership, recv_rows), gram_part(unit_rows, membership, centroids)), "row"
    )
    diag_term = perp_weight * member_counts.astype(jnp.float32)[:, None] + prior_weight
    residual = (
        aniso_par * row_sums
        + prior_weight * centroids
        - (diag_term * centroids + (aniso_par - perp_weight) * first_gram)
    )
    direction = residual
    norm_now = jnp.sum(residual * residual, axis=1, keepdims=True)
    for iteration in range(ITERS):
        applied = diag_term * direction + (aniso_par - perp_weight) * lax.psum(
            gram_part(unit_rows, membership, direction), "row"
        )
        step_len = norm_now / jnp.sum(direction * applied, axis=1, keepdims=True)
        centroids = centroids + step_len * direction
        residual = residual - step_len * applied
        norm_next = jnp.sum(residual * residual, axis=1, keepdims=True)
        direction = residual + norm_next / norm_now * direction
        norm_now = norm_next
    panel = centroids.astype(jnp.bfloat16)
    start_score = jnp.full((next_rows.shape[0],), -jnp.inf, jnp.float32)
    piece = lax.all_gather(panel, "list", axis=0, tiled=True)
    piece_rows = piece.shape[0]
    block_size = 512
    blocks = piece.reshape(piece_rows // block_size, block_size, piece.shape[1])

    def one_block(running, piece_block):
        scores = lax.dot_general(
            next_rows, piece_block, (((1,), (1,)), ((), ())), preferred_element_type=jnp.float32
        )
        return (jnp.maximum(running, jnp.max(scores, axis=1)), None)

    result, unused = lax.scan(one_block, start_score, blocks)
    return (centroids, result / width)


def solution(mesh):
    in_specs = (
        P(("list", "row"), None),
        P(("list", "row")),
        P(),
        P("list"),
        P("list", None),
        P(("list", "row"), None),
    )
    out_specs = (P("list", None), P(("list", "row")))
    return jax.shard_map(
        on_device, mesh=mesh, in_specs=in_specs, out_specs=out_specs, check_vma=False
    )
```

profile of v0, /device:TPU:1, one launch (start us, length us, event | category | flops | bytes accessed | tf_op | source)
XLA Modules:
  0.0 470.4 jit_solution(17790374509922220616)
XLA Ops:
  7.2 0.8 fusion.41
  7.9 6.1 %gather_fusion = s32[1024]{0:T(1024)S(1)} fusion(s32[4096]{0:T(1024)S(1)} %copy-done, s32[1024]{0:T(1024)S(1)} %fusion.41), kind=kCustom, calls=%fused_computation | custom fusion | bytes 12288 | tf_op jit(solution)/shard_map/jit(_take)/gather | solution.py:64
  14.2 18.0 %reduce-window.6 = s32[64,8,128]{2,1,0:T(8,128)S(1)} reduce-window(s32[64,8,128]{2,1,0:T(8,128)S(1)} %fusion.11, s32[]{:T(128)} %constant.69.clone.1), window={size=1x1x128 pad=0_0x0_0x127_0}, to_apply=%region_0.1 | reduce-window | flops 8323072 | bytes 524292 | tf_op jit(solution)/shard_map/reduce-window
  32.8 4.3 scatter_custom_fusion
  37.1 0.7 all_to_all.9
  37.8 10.3 %all-to-all-start = ((s32[64,1,24]{2,1,0:T(1,128)}), s32[64,1,24]{2,1,0:T(1,128)S(1)}, u32[]{:S(2)}, u32[]{:S(2)}) async-start(s32[64,1,24]{2,1,0:T(1,128)} %bitcast.3), calls=%async_computation | async-start | bytes 65536 | tf_op jit(solution)/shard_map/all_to_all | solution.py:84
  48.2 7.5 %scatter_custom_fusion.1 = bf16[1536,768]{1,0:T(8,128)(2,1)} fusion(s32[1024]{0:T(1024)S(1)} %compare_select_fusion, bf16[1024,768]{1,0:T(8,128)(2,1)} %param.8, bf16[]{:T(256)} %constant.79.clone.1), kind=kCustom, calls=%fused_computation.18 | custom fusion | bytes 2359808 | tf_op jit(solution)/shard_map/scatter | solution.py:73
  55.9 8.6 %all-to-all-start.1 = ((bf16[64,24,768]{2,1,0:T(8,128)(2,1)}), bf16[64,24,768]{2,1,0:T(8,128)(2,1)S(1)}, u32[]{:S(2)}, u32[]{:S(2)}) async-start(bf16[64,24,768]{2,1,0:T(8,128)(2,1)} %bitcast.46), calls=%async_computation.1 | async-start | bytes 4718592 | tf_op jit(solution)/shard_map/all_to_all | solution.py:83
  65.1 0.7 reduce.5
  65.9 29.0 %all-to-all-done.1 = bf16[64,24,768]{2,1,0:T(8,128)(2,1)S(1)} async-done(((bf16[64,24,768]{2,1,0:T(8,128)(2,1)}), bf16[64,24,768]{2,1,0:T(8,128)(2,1)S(1)}, u32[]{:S(2)}, u32[]{:S(2)}) %all-to-all-start.1) | async-done | bytes 2359328 | tf_op jit(solution)/shard_map/all_to_all | solution.py:83
  95.5 0.9 copy-done.1
  96.5 2.2 divide_convert_fusion
  98.7 0.8 fusion.36
  99.5 0.8 fusion.6
  100.9 1.2 convolution_add_fusion.7
  102.1 1.2 fusion.12
  103.6 52.9 %all-reduce.12.cloned.1.call-done = (f32[64,768]{1,0:T(8,128)}, f32[64,768]{1,0:T(8,128)}) async-done(((f32[64,768]{1,0:T(8,128)}, f32[64,768]{1,0:T(8,128)}), (f32[64,768]{1,0:T(8,128)}, f32[64,768]{1,0:T(8,128)})) %all-reduce.12.cloned.1.call-update) | async-done | bytes 393232 | tf_op jit(solution)/shard_map/psum | solution.py:90
  156.4 1.1 add_subtract_fusion
  157.6 0.8 fusion.33
  158.4 0.8 fusion.5
  159.7 1.2 convolution_add_fusion.6
  161.0 49.5 %all-reduce.6.cloned.1.call-done = f32[64,768]{1,0:T(8,128)} async-done(((f32[64,768]{1,0:T(8,128)}), f32[64,768]{1,0:T(8,128)}) %all-reduce.6.cloned.1.call-update) | async-done | bytes 196624 | tf_op jit(solution)/shard_map/psum | solution.py:102
  210.5 1.1 multiply_reduce_fusion.5
  211.7 1.1 multiply_reduce_fusion.4
  212.9 0.8 fusion.30
  213.8 0.8 fusion.4
  215.1 1.2 convolution_add_fusion.5
  216.4 49.2 %all-reduce.8.cloned.1.call-done = f32[64,768]{1,0:T(8,128)} async-done(((f32[64,768]{1,0:T(8,128)}), f32[64,768]{1,0:T(8,128)}) %all-reduce.8.cloned.1.call-update) | async-done | bytes 196624 | tf_op jit(solution)/shard_map/psum | solution.py:102
  265.6 1.1 multiply_reduce_fusion.3
  266.8 1.1 multiply_reduce_fusion.2
  267.9 1.1 multiply_add_fusion.1
  269.0 0.8 fusion.27
  269.8 0.8 fusion.3
  271.2 1.2 convolution_add_fusion.4
  272.5 49.3 %all-reduce.10.cloned.1.call-done = f32[64,768]{1,0:T(8,128)} async-done(((f32[64,768]{1,0:T(8,128)}), f32[64,768]{1,0:T(8,128)}) %all-reduce.10.cloned.1.call-update) | async-done | bytes 196624 | tf_op jit(solution)/shard_map/psum | solution.py:102
  321.8 1.1 multiply_reduce_fusion.1
  322.9 0.8 fusion.43
  323.7 112.5 %all-gather.2.cloned.1.call-done = bf16[4096,768]{1,0:T(8,128)(2,1)} async-done(((bf16[64,768]{1,0:T(8,128)(2,1)}), bf16[4096,768]{1,0:T(8,128)(2,1)}) %all-gather.2.cloned.1.call-update) | async-done | bytes 6291472 | tf_op jit(solution)/shard_map/all_gather | solution.py:113
  436.2 27.1 %while.11 = (s32[]{:T(128)}, f32[1536]{0:T(1024)S(1)}, bf16[8,512,768]{2,1,0:T(8,128)(2,1)}, bf16[1536,768]{1,0:T(8,128)(2,1)}, s32[]{:T(128)}, /*index=5*/s32[]{:T(128)}) while((s32[]{:T(128)}, f32[1536]{0:T(1024)S(1)}, bf16[8,512,768]{2,1,0:T(8,128)(2,1)}, bf16[1536,768]{1,0:T(8,128)(2,1)}, s32[]{:T(128)}, ...), condition=%wide.region_19.20_spmd.clone, body=%wide.region_17.19_spmd.clone.sunk | while | flops 1208747520 | bytes 3170895 | solution.py:124
  436.2 3.3 convolution_reduce_fusion.2
  439.6 3.3 convolution_reduce_fusion.2
  443.0 3.3 convolution_reduce_fusion.2
  446.4 3.3 convolution_reduce_fusion.2
  449.8 3.3 convolution_reduce_fusion.2
  453.2 3.3 convolution_reduce_fusion.2
  456.5 3.3 convolution_reduce_fusion.2
  459.9 3.3 convolution_reduce_fusion.2
  463.3 0.6 broadcast_multiply_fusion
  (57 shorter events, 4.9 us)
Async XLA Ops:
  7.2 0.8 copy-start
  7.2 6.9 %copy-start.4 = (s32[1024]{0:T(1024)S(1)}, s32[1024]{0:T(1024)}, u32[]{:S(2)}) copy-start(s32[1024]{0:T(1024)} %param.9) | copy-start | bytes 12292
  37.8 18.1 %all-to-all-start = ((s32[64,1,24]{2,1,0:T(1,128)}), s32[64,1,24]{2,1,0:T(1,128)S(1)}, u32[]{:S(2)}, u32[]{:S(2)}) async-start(s32[64,1,24]{2,1,0:T(1,128)} %bitcast.3), calls=%async_computation | async-start | bytes 65536 | tf_op jit(solution)/shard_map/all_to_all | solution.py:84
  55.9 39.0 %all-to-all-start.1 = ((bf16[64,24,768]{2,1,0:T(8,128)(2,1)}), bf16[64,24,768]{2,1,0:T(8,128)(2,1)S(1)}, u32[]{:S(2)}, u32[]{:S(2)}) async-start(bf16[64,24,768]{2,1,0:T(8,128)(2,1)} %bitcast.46), calls=%async_computation.1 | async-start | bytes 4718592 | tf_op jit(solution)/shard_map/all_to_all | solution.py:83
  64.6 91.9 %all-reduce.12.cloned.1.call-start = ((), (), s32[]{:S(2)}) async-start(), calls=%async_computation.6 | async-start | bytes 786432 | tf_op jit(solution)/shard_map/psum | solution.py:90
  95.0 1.4 copy-start.1
  96.5 2.2 copy-start.3
  100.4 1.7 copy-start.2
  100.9 2.7 copy-start.5
  103.3 107.2 %all-reduce.6.cloned.1.call-start = ((), (), s32[]{:S(2)}) async-start(), calls=%async_computation.2 | async-start | bytes 393216 | tf_op jit(solution)/shard_map/psum | solution.py:102
  161.0 104.7 %all-reduce.8.cloned.1.call-start = ((), (), s32[]{:S(2)}) async-start(), calls=%async_computation.3 | async-start | bytes 393216 | tf_op jit(solution)/shard_map/psum | solution.py:102
  216.3 105.4 %all-reduce.10.cloned.1.call-start = ((), (), s32[]{:S(2)}) async-start(), calls=%async_computation.4 | async-start | bytes 393216 | tf_op jit(solution)/shard_map/psum | solution.py:102
  272.4 163.8 %all-gather.2.cloned.1.call-start = ((), (), s32[]{:S(2)}) async-start(), calls=%async_computation.5 | async-start | bytes 6389760 | tf_op jit(solution)/shard_map/all_gather | solution.py:113
Sparse Core Ops, SparseCore 0:
  103.5 52.9 all-reduce.11
  161.1 49.3 all-reduce.5
  216.5 49.1 all-reduce.7
  272.5 49.1 all-reduce.9
  323.9 112.3 all-gather.1
where the time goes:
time: 471 us; the launch traced here: 470 us
  waiting for transfers between devices  343 us (73%)
  matrix products  41.5 us (9%)
  other arithmetic  31.9 us (7%)
  local copies, waits for them, and re-layouts  20.6 us (4%)
  starting transfers between devices  19.3 us (4%)
  between operations  14.1 us (3%)
    psum x3, waiting for transfers between devices, on_device(): lax.psum(gram_part(unit_rows, membership, direction), 'row')  148 us
    all_gather x1, waiting for transfers between devices, on_device(): piece = lax.all_gather(panel, 'list', axis=0, tiled=True)  112 us
    psum x1, waiting for transfers between devices, on_device(): lax.psum((member_total(membership, recv_rows), gram_part(unit_rows, membe...  52.9 us
    all_to_all x1, waiting for transfers between devices, on_device(): lax.all_to_all(send_rows, 'list', split_axis=0, concat_axis=0, tiled=True)  29 us
    dot_general x8, matrix products, one_block(): lax.dot_general(next_rows, piece_block, (((1,), (1,)), ((), ())), preferr...  26.8 us
    another operation x2, other arithmetic  18 us
    all_to_all x1, starting transfers between devices, on_device(): lax.all_to_all(send_local, 'list', split_axis=0, concat_axis=0, tiled=True)  10.3 us
  transfers between devices with their start and end apart: 7, of which 7 were waited for; matrix products, arithmetic and copies ran while one was open for 2% of the time, Pallas kernels for 0%

commit v1 on v0

--- a/solution.py
+++ b/solution.py
@@ -110,7 +110,9 @@
         norm_now = norm_next
     panel = centroids.astype(jnp.bfloat16)
     start_score = jnp.full((next_rows.shape[0],), -jnp.inf, jnp.float32)
-    piece = lax.all_gather(panel, "list", axis=0, tiled=True)
+    piece = jnp.concatenate(
+        lax.all_to_all(jnp.stack([panel] * lax.axis_size("list")), "list", 0, 0), axis=0
+    )
     piece_rows = piece.shape[0]
     block_size = 512
     blocks = piece.reshape(piece_rows // block_size, block_size, piece.shape[1])

time: 471 us -> 451 us (0.958); the launches traced: 470 us -> 442 us
  waiting for transfers between devices: 343 us -> 307 us
  starting transfers between devices: 19.3 us -> 29.7 us
  matrix products: 41.5 us -> 35.2 us
    all_gather x1 -> x0, waiting for transfers between devices: 112 us -> none  [on_device(): piece = lax.all_gather(panel, 'list', axis=0, tiled=True)]
    all_to_all x0 -> x1, waiting for transfers between devices: none -> 76.9 us  [on_device(): lax.all_to_all(jnp.stack([panel] * lax.axis_size('list')), 'list', 0, 0)]
    all_to_all x0 -> x1, starting transfers between devices: none -> 10.4 us  [on_device(): lax.all_to_all(jnp.stack([panel] * lax.axis_size('list')), 'list', 0, 0)]
    dot_general x8, matrix products: 26.8 us -> 20.5 us  [one_block(): lax.dot_general(next_rows, piece_block, (((1,), (1,)), ((), ())), preferr...]
where the time goes in v1:
time: 451 us; the launch traced here: 442 us
  waiting for transfers between devices  307 us (68%)
  matrix products  35.2 us (8%)
  other arithmetic  31.9 us (7%)
  starting transfers between devices  29.7 us (7%)
  local copies, waits for them, and re-layouts  24 us (5%)
  between operations  14.1 us (3%)
    psum x3, waiting for transfers between devices, on_device(): lax.psum(gram_part(unit_rows, membership, direction), 'row')  148 us
    all_to_all x1, waiting for transfers between devices, on_device(): lax.all_to_all(jnp.stack([panel] * lax.axis_size('list')), 'list', 0, 0)  76.9 us
    psum x1, waiting for transfers between devices, on_device(): lax.psum((member_total(membership, recv_rows), gram_part(unit_rows, membe...  52.9 us
    all_to_all x1, waiting for transfers between devices, on_device(): lax.all_to_all(send_rows, 'list', split_axis=0, concat_axis=0, tiled=True)  29 us
    dot_general x8, matrix products, one_block(): lax.dot_general(next_rows, piece_block, (((1,), (1,)), ((), ())), preferr...  20.5 us
    another operation x2, other arithmetic  18 us
    all_to_all x1, starting transfers between devices, on_device(): lax.all_to_all(jnp.stack([panel] * lax.axis_size('list')), 'list', 0, 0)  10.4 us
    all_to_all x1, starting transfers between devices, on_device(): lax.all_to_all(send_local, 'list', split_axis=0, concat_axis=0, tiled=True)  10.3 us
  transfers between devices with their start and end apart: 7, of which 7 were waited for; matrix products, arithmetic and copies ran while one was open for 2% of the time, Pallas kernels for 0%

profile of v1, /device:TPU:1, one launch (start us, length us, event | category | flops | bytes accessed | tf_op | source)
XLA Modules:
  0.0 442.3 jit_solution(16413994300570559885)
XLA Ops:
  7.2 0.8 fusion.41
  7.9 6.1 %gather_fusion = s32[1024]{0:T(1024)S(1)} fusion(s32[4096]{0:T(1024)S(1)} %copy-done, s32[1024]{0:T(1024)S(1)} %fusion.41), kind=kCustom, calls=%fused_computation | custom fusion | bytes 12288 | tf_op jit(solution)/shard_map/jit(_take)/gather | solution.py:64
  14.2 18.0 %reduce-window.6 = s32[64,8,128]{2,1,0:T(8,128)S(1)} reduce-window(s32[64,8,128]{2,1,0:T(8,128)S(1)} %fusion.11, s32[]{:T(128)} %constant.69.clone.1), window={size=1x1x128 pad=0_0x0_0x127_0}, to_apply=%region_0.1 | reduce-window | flops 8323072 | bytes 524292 | tf_op jit(solution)/shard_map/reduce-window
  32.8 4.3 scatter_custom_fusion
  37.8 10.3 %all-to-all-start = ((s32[64,1,24]{2,1,0:T(1,128)}), s32[64,1,24]{2,1,0:T(1,128)S(1)}, u32[]{:S(2)}, u32[]{:S(2)}) async-start(s32[64,1,24]{2,1,0:T(1,128)} %bitcast.3), calls=%async_computation | async-start | bytes 65536 | tf_op jit(solution)/shard_map/all_to_all | solution.py:84
  48.2 7.5 %scatter_custom_fusion.1 = bf16[1536,768]{1,0:T(8,128)(2,1)} fusion(s32[1024]{0:T(1024)S(1)} %compare_select_fusion, bf16[1024,768]{1,0:T(8,128)(2,1)} %param.8, bf16[]{:T(256)} %constant.79.clone.1), kind=kCustom, calls=%fused_computation.18 | custom fusion | bytes 2359808 | tf_op jit(solution)/shard_map/scatter | solution.py:73
  55.9 8.6 %all-to-all-start.1 = ((bf16[64,24,768]{2,1,0:T(8,128)(2,1)}), bf16[64,24,768]{2,1,0:T(8,128)(2,1)S(1)}, u32[]{:S(2)}, u32[]{:S(2)}) async-start(bf16[64,24,768]{2,1,0:T(8,128)(2,1)} %bitcast.46), calls=%async_computation.1 | async-start | bytes 4718592 | tf_op jit(solution)/shard_map/all_to_all | solution.py:83
  65.1 0.7 reduce.5
  65.9 29.0 %all-to-all-done.1 = bf16[64,24,768]{2,1,0:T(8,128)(2,1)S(1)} async-done(((bf16[64,24,768]{2,1,0:T(8,128)(2,1)}), bf16[64,24,768]{2,1,0:T(8,128)(2,1)S(1)}, u32[]{:S(2)}, u32[]{:S(2)}) %all-to-all-start.1) | async-done | bytes 2359328 | tf_op jit(solution)/shard_map/all_to_all | solution.py:83
  95.5 0.9 copy-done.1
  96.5 2.2 divide_convert_fusion
  98.7 0.8 fusion.36
  99.5 0.8 fusion.6
  100.9 1.2 convolution_add_fusion.7
  102.1 1.2 fusion.12
  103.6 52.9 %all-reduce.12.cloned.1.call-done = (f32[64,768]{1,0:T(8,128)}, f32[64,768]{1,0:T(8,128)}) async-done(((f32[64,768]{1,0:T(8,128)}, f32[64,768]{1,0:T(8,128)}), (f32[64,768]{1,0:T(8,128)}, f32[64,768]{1,0:T(8,128)})) %all-reduce.12.cloned.1.call-update) | async-done | bytes 393232 | tf_op jit(solution)/shard_map/psum | solution.py:90
  156.4 1.1 add_subtract_fusion
  157.6 0.8 fusion.33
  158.4 0.8 fusion.5
  159.7 1.2 convolution_add_fusion.6
  161.0 49.5 %all-reduce.6.cloned.1.call-done = f32[64,768]{1,0:T(8,128)} async-done(((f32[64,768]{1,0:T(8,128)}), f32[64,768]{1,0:T(8,128)}) %all-reduce.6.cloned.1.call-update) | async-done | bytes 196624 | tf_op jit(solution)/shard_map/psum | solution.py:102
  210.5 1.1 multiply_reduce_fusion.5
  211.7 1.1 multiply_reduce_fusion.4
  212.9 0.8 fusion.30
  213.8 0.8 fusion.4
  215.1 1.2 convolution_add_fusion.5
  216.4 49.2 %all-reduce.8.cloned.1.call-done = f32[64,768]{1,0:T(8,128)} async-done(((f32[64,768]{1,0:T(8,128)}), f32[64,768]{1,0:T(8,128)}) %all-reduce.8.cloned.1.call-update) | async-done | bytes 196624 | tf_op jit(solution)/shard_map/psum | solution.py:102
  265.6 1.1 multiply_reduce_fusion.3
  266.8 1.1 multiply_reduce_fusion.2
  267.9 1.1 multiply_add_fusion.1
  269.0 0.8 fusion.27
  269.8 0.8 fusion.3
  271.2 1.2 convolution_add_fusion.4
  272.4 49.3 %all-reduce.10.cloned.1.call-done = f32[64,768]{1,0:T(8,128)} async-done(((f32[64,768]{1,0:T(8,128)}), f32[64,768]{1,0:T(8,128)}) %all-reduce.10.cloned.1.call-update) | async-done | bytes 196624 | tf_op jit(solution)/shard_map/psum | solution.py:102
  321.8 1.1 multiply_reduce_fusion.1
  322.9 0.8 fusion.43
  323.7 3.4 stack.2
  327.1 10.4 %all-to-all-start.2 = ((bf16[64,64,768]{2,1,0:T(8,128)(2,1)}), bf16[64,64,768]{2,1,0:T(8,128)(2,1)}, u32[]{:S(2)}, u32[]{:S(2)}) async-start(bf16[64,64,768]{2,1,0:T(8,128)(2,1)} %stack.2), calls=%async_computation.2 | async-start | bytes 12582912 | tf_op jit(solution)/shard_map/all_to_all | solution.py:114
  337.5 76.9 %all-to-all-done.2 = bf16[64,64,768]{2,1,0:T(8,128)(2,1)} async-done(((bf16[64,64,768]{2,1,0:T(8,128)(2,1)}), bf16[64,64,768]{2,1,0:T(8,128)(2,1)}, u32[]{:S(2)}, u32[]{:S(2)}) %all-to-all-start.2) | async-done | bytes 6291488 | tf_op jit(solution)/shard_map/all_to_all | solution.py:114
  414.4 20.8 %while.11 = (s32[]{:T(128)}, f32[1536]{0:T(1024)S(1)}, bf16[8,512,768]{2,1,0:T(8,128)(2,1)}, bf16[1536,768]{1,0:T(8,128)(2,1)S(1)}, s32[]{:T(128)}, /*index=5*/s32[]{:T(128)}) while((s32[]{:T(128)}, f32[1536]{0:T(1024)S(1)}, bf16[8,512,768]{2,1,0:T(8,128)(2,1)}, bf16[1536,768]{1,0:T(8,128)(2,1)S(1)}, s32[]{:T(128)}, ...), condition=%wide.region_19.20_spmd.clone, body=%wide.region_17.19_spmd.clone.sunk | while | flops 1208747520 | bytes 3170895 | solution.py:126
  414.4 2.6 convolution_reduce_fusion.2
  417.0 2.6 convolution_reduce_fusion.2
  419.6 2.6 convolution_reduce_fusion.2
  422.2 2.6 convolution_reduce_fusion.2
  424.8 2.6 convolution_reduce_fusion.2
  427.4 2.6 convolution_reduce_fusion.2
  430.0 2.6 convolution_reduce_fusion.2
  432.6 2.6 convolution_reduce_fusion.2
  (59 shorter events, 6.1 us)
Async XLA Ops:
  7.2 0.8 copy-start
  7.2 6.9 %copy-start.4 = (s32[1024]{0:T(1024)S(1)}, s32[1024]{0:T(1024)}, u32[]{:S(2)}) copy-start(s32[1024]{0:T(1024)} %param.9) | copy-start | bytes 12292
  37.8 18.1 %all-to-all-start = ((s32[64,1,24]{2,1,0:T(1,128)}), s32[64,1,24]{2,1,0:T(1,128)S(1)}, u32[]{:S(2)}, u32[]{:S(2)}) async-start(s32[64,1,24]{2,1,0:T(1,128)} %bitcast.3), calls=%async_computation | async-start | bytes 65536 | tf_op jit(solution)/shard_map/all_to_all | solution.py:84
  55.9 39.0 %all-to-all-start.1 = ((bf16[64,24,768]{2,1,0:T(8,128)(2,1)}), bf16[64,24,768]{2,1,0:T(8,128)(2,1)S(1)}, u32[]{:S(2)}, u32[]{:S(2)}) async-start(bf16[64,24,768]{2,1,0:T(8,128)(2,1)} %bitcast.46), calls=%async_computation.1 | async-start | bytes 4718592 | tf_op jit(solution)/shard_map/all_to_all | solution.py:83
  64.6 91.9 %all-reduce.12.cloned.1.call-start = ((), (), s32[]{:S(2)}) async-start(), calls=%async_computation.6 | async-start | bytes 786432 | tf_op jit(solution)/shard_map/psum | solution.py:90
  95.0 1.4 copy-start.1
  96.5 2.2 copy-start.3
  100.4 1.7 copy-start.2
  100.9 2.7 copy-start.6
  103.3 107.2 %all-reduce.6.cloned.1.call-start = ((), (), s32[]{:S(2)}) async-start(), calls=%async_computation.3 | async-start | bytes 393216 | tf_op jit(solution)/shard_map/psum | solution.py:102
  161.0 104.7 %all-reduce.8.cloned.1.call-start = ((), (), s32[]{:S(2)}) async-start(), calls=%async_computation.4 | async-start | bytes 393216 | tf_op jit(solution)/shard_map/psum | solution.py:102
  216.3 105.4 %all-reduce.10.cloned.1.call-start = ((), (), s32[]{:S(2)}) async-start(), calls=%async_computation.5 | async-start | bytes 393216 | tf_op jit(solution)/shard_map/psum | solution.py:102
  327.1 87.3 %copy-start.5 = (bf16[1536,768]{1,0:T(8,128)(2,1)S(1)}, bf16[1536,768]{1,0:T(8,128)(2,1)}, u32[]{:S(2)}) copy-start(bf16[1536,768]{1,0:T(8,128)(2,1)} %param.13) | copy-start | bytes 7077892
  327.1 87.3 %all-to-all-start.2 = ((bf16[64,64,768]{2,1,0:T(8,128)(2,1)}), bf16[64,64,768]{2,1,0:T(8,128)(2,1)}, u32[]{:S(2)}, u32[]{:S(2)}) async-start(bf16[64,64,768]{2,1,0:T(8,128)(2,1)} %stack.2), calls=%async_computation.2 | async-start | bytes 12582912 | tf_op jit(solution)/shard_map/all_to_all | solution.py:114
Sparse Core Ops, SparseCore 0:
  103.5 52.9 all-reduce.11
  161.1 49.3 all-reduce.5
  216.5 49.1 all-reduce.7
  272.5 49.1 all-reduce.9
